TPU v7x, 32 devices: a whole 2x2x4 slice. The times are simulated.
32 devices in a mesh: mesh: 4 (over y, core), mode: 8 (over z, x).
Axes of the slice: x: 2, y: 2, z: 4, core: 2. Of those that a mesh axis runs over, the one named last changes fastest.
Arguments:
- field: float32 [256, 512, 1024], P('mode', 'mesh'), may hold values from -6 to 6
- kappa: bfloat16 [3, 512, 1024], P(None, ('mesh', 'mode')), may hold values from 0.099609375 to 1
- mass: float32 [512, 1024], P(('mesh', 'mode')), may hold values from 0.5 to 1.5
- kl_modes: bfloat16 [3, 256, 256], replicated, may hold values from -0.375 to 0.375
- to_points: bfloat16 [512, 256], replicated, may hold values from -0.375 to 0.375
- from_points: bfloat16 [256, 512], replicated, may hold values from -0.25 to 0.25
- capacity: float32 [512], replicated, may hold values from 0.5 to 2
- latent: float32 [512], replicated, may hold values from 0.5 to 3
Outputs:
- residual: bfloat16 [256, 512, 1024], P('mode', 'mesh')
All inputs are finite; a program needn't handle non-finite values.
Results may differ from a plain program's by a relative error of at most 0.0058.
Values may be sent and summed in bfloat16 or wider, within the bound.
A program may use at most 256 MiB of HBM per device.

v0:
```python
import jax
import jax.numpy as jnp
from jax import lax
from jax.sharding import PartitionSpec as P


def extended(cells, sides, width):
    for axis, dim in sides:
        count = lax.axis_size(axis)
        ends = count - 1
        head = lax.slice_in_dim(cells, 0, width, axis=dim)
        tail = lax.slice_in_dim(cells, cells.shape[dim] - width, cells.shape[dim], axis=dim)
        cells = jnp.concatenate(
            [
                lax.ppermute(tail, axis, [(i, (i + 1) % count) for i in range(ends)]),
                cells,
                lax.ppermute(head, axis, [((i + 1) % count, i) for i in range(ends)]),
            ],
            axis=dim,
        )
    return cells


def conduct(values, kappa):
    count = values.shape[1] - 2
    width = values.shape[2]
    vals = jnp.pad(values.astype(jnp.float32), ((0, 0), (0, 0), (1, 1)))[None]
    kaps = jnp.pad(kappa.astype(jnp.float32), ((0, 0), (0, 0), (1, 1)))[:, None]
    centre = vals[:, :, 1 : 1 + count, 1 : 1 + width]
    kcentre = kaps[:, :, 1 : 1 + count, 1 : 1 + width]
    total = jnp.zeros((kaps.shape[0], vals.shape[1], count, width), jnp.float32)
    for shift_x, shift_y in ((0, 1), (2, 1), (1, 0), (1, 2)):
        other = vals[:, :, shift_x : shift_x + count, shift_y : shift_y + width]
        kother = kaps[:, :, shift_x : shift_x + count, shift_y : shift_y + width]
        total = total + 0.5 * (kcentre + kother) * (centre - other)
    return total.astype(jnp.bfloat16)


def finish(coarse, images, mass_rows, kl_modes, to_points, from_points, capacity, latent):
    mixed = jnp.einsum("kij,kjxy->ixy", kl_modes, images, preferred_element_type=jnp.float32)
    temps = jnp.einsum("qi,ixy->qxy", to_points, coarse, preferred_element_type=jnp.float32)
    heat = (
        capacity[:, None, None] * temps + latent[:, None, None] * jax.nn.sigmoid(2.0 * temps)
    ).astype(jnp.bfloat16)
    enthalpy = jnp.einsum("iq,qxy->ixy", from_points, heat, preferred_element_type=jnp.float32)
    return (mass_rows[None] * enthalpy + mixed).astype(jnp.bfloat16)


def body(field, kappa, mass, kl_modes, to_points, from_points, capacity, latent):
    coarse = field.astype(jnp.bfloat16)
    owned = coarse.shape[0]
    width = coarse.shape[2]
    groups = lax.axis_size("mode")
    terms = kappa.shape[0]
    kap_rows = lax.all_gather(kappa, "mode", axis=1, tiled=True)
    stacked = jnp.concatenate([coarse, kap_rows], 0)
    padded = extended(stacked, (("mesh", 1),), 1)
    images = conduct(padded[:owned], padded[owned:])
    joined = jnp.concatenate([coarse[None], images], 0)
    joined = joined.reshape((terms + 1) * owned, coarse.shape[1], width)
    moved = lax.all_to_all(joined, "mode", split_axis=1, concat_axis=0, tiled=True)
    node_rows = moved.shape[1]
    moved = moved.reshape(groups, terms + 1, owned, node_rows, width)
    moved = jnp.transpose(moved, (1, 0, 2, 3, 4)).reshape(
        terms + 1, groups * owned, node_rows, width
    )
    node_coarse = moved[0]
    node_images = moved[1:]
    result = finish(
        node_coarse, node_images, mass, kl_modes, to_points, from_points, capacity, latent
    )
    return lax.all_to_all(result, "mode", split_axis=0, concat_axis=1, tiled=True)


def solution(mesh):
    in_specs = (
        P("mode", "mesh", None),
        P(None, ("mesh", "mode"), None),
        P(("mesh", "mode"), None),
        P(),
        P(),
        P(),
        P(),
        P(),
    )
    out_specs = P("mode", "mesh", None)
    return jax.shard_map(body, mesh=mesh, in_specs=in_specs, out_specs=out_specs, check_vma=False)
```

profile of v0, /device:TPU:1, one launch (start us, length us, event | category | flops | bytes accessed | tf_op | source)
XLA Modules:
  0.0 1315.9 jit_solution(11272950333644281777)
XLA Ops:
  0.0 16.5 %copy.54 = bf16[32,128,1024]{2,0,1:T(8,128)(2,1)S(1)} copy(f32[32,128,1024]{2,1,0:T(8,128)} %param.8) | data formatting | bytes 25165824 | tf_op args[0]
  16.6 28.1 %all_gather.3 = bf16[3,128,1024]{2,1,0:T(8,128)(2,1)S(1)} all-gather(bf16[3,16,1024]{2,1,0:T(8,128)(2,1)S(1)} %copy-done.2), channel_id=1, replica_groups=mesh['mesh'=4,'mode'=8] {'mode'}, dimensions={1}, use_global_device_ids=true | all-gather | bytes 884736 | tf_op jit(solution)/shard_map/all_gather | solution.py:55
  44.6 0.7 copy.32
  45.3 0.0 slice-start.3
  45.4 9.1 collective-permute-start
  54.5 2.1 collective-permute-start.1
  56.7 11.4 copy.56
  68.1 12.0 fusion.11
  80.1 51.1 %fusion.6 = (f32[32,128,1024]{2,0,1:T(8,128)}, f32[32,128,1024]{2,0,1:T(8,128)}, f32[32,128,1024]{2,0,1:T(8,128)}, f32[32,128,1024]{2,0,1:T(8,128)}) fusion(f32[1,32,130,1026]{3,1,2,0:T(8,128)} %fusion.11), kind=kLoop, calls=%fused_computation.15 | loop fusion | flops 16777216 | bytes 150994944 | tf_op jit(solution)/shard_map/mul | solution.py:35
  131.2 2.9 fusion.38
  134.1 4.5 fusion.36
  138.7 46.6 %add_convert_fusion = bf16[3,32,128,1024]{3,1,0,2:T(8,128)(2,1)} fusion(f32[32,128,1024]{2,0,1:T(8,128)} %get-tuple-element.8, f32[3,128,1024]{2,0,1:T(4,128)S(1)} %get-tuple-element.14, f32[32,128,1024]{2,0,1:T(8,128)} %get-tuple-element.6, f32[3,128,1024]{2,0,1:T(4,128)S(1)} %get-tuple-element.12, f32[32,128,1024]{2,0,1:T(8,128)} %get-tuple-element.7, ...), kind=kLoop, calls=%fused_computation | loop fusion | flops 100663296 | bytes 98566144 | tf_op jit(solution)/shard_map/convert_element_type | solution.py:36
  185.3 23.1 %pad_maximum_fusion = bf16[4,32,128,1024]{3,1,0,2:T(8,128)(2,1)} fusion(bf16[3,32,128,1024]{3,1,0,2:T(8,128)(2,1)} %add_convert_fusion, bf16[1,32,128,1024]{3,1,0,2:T(8,128)(2,1)} %bitcast.79), kind=kLoop, calls=%fused_computation.1 | loop fusion | flops 16777216 | bytes 67108864 | tf_op jit(solution)/shard_map/concatenate | solution.py:59
  208.4 733.1 %all_to_all.33 = bf16[128,128,1024]{2,0,1:T(8,128)(2,1)} all-to-all(bf16[128,128,1024]{2,0,1:T(8,128)(2,1)} %bitcast.72), channel_id=1, replica_groups=mesh['mesh'=4,'mode'=8] {'mode'}, dimensions={1} | all-to-all | bytes 67108864 | tf_op jit(solution)/shard_map/all_to_all | solution.py:61
  941.5 30.8 %copy.35 = bf16[8,128,16,1024]{3,2,1,0:T(8,128)(2,1)} copy(bf16[8,128,16,1024]{3,1,2,0:T(8,128)(2,1)} %bitcast.73) | data formatting | bytes 67108864 | tf_op jit(solution)/shard_map/all_to_all | solution.py:61
  972.3 21.4 %slice.80 = bf16[3,8,32,16,1024]{4,3,2,0,1:T(8,128)(2,1)} slice(bf16[4,8,32,16,1024]{4,3,2,0,1:T(8,128)(2,1)} %bitcast.70), slice={[1:4], [0:8], [0:32], [0:16], [0:1024]} | slice | bytes 50331648 | tf_op jit(solution)/shard_map/slice | solution.py:68
  993.7 8.7 slice.79
  1002.4 21.3 %copy.37 = bf16[3,8,32,16,1024]{4,3,2,1,0:T(8,128)(2,1)} copy(bf16[3,8,32,16,1024]{4,3,2,0,1:T(8,128)(2,1)} %slice.80) | data formatting | bytes 50331648 | tf_op jit(solution)/shard_map/slice | solution.py:68
  1023.8 0.0 copy-start.6
  1023.8 59.9 %fusion = f32[16,1024,256,1]{2,1,3,0:T(8,128)} fusion(bf16[3,256,16,1024]{3,2,1,0:T(8,128)(2,1)} %bitcast.80, bf16[3,256,256]{2,1,0:T(8,128)(2,1)S(1)} %copy-done), kind=kOutput, calls=%fused_computation.5 | convolution fusion | flops 6442450944 | bytes 42336256 | tf_op jit(solution)/shard_map/kij,kjxy->ixy/dot_general | solution.py:40
  1083.8 22.9 %fusion.23 = bf16[256,16,1024]{0,2,1:T(8,128)(2,1)} fusion(f32[16,1024,256,1]{2,1,3,0:T(8,128)} %fusion, f32[512]{0:T(512)S(1)} %copy-done.6, f32[512]{0:T(512)S(1)} %copy-done.7, bf16[256,16,1024]{2,1,0:T(8,128)(2,1)} %bitcast.81, f32[16,1024]{1,0:T(8,128)S(1)} %copy-done.5, bf16[256,512]{1,0:T(8,128)(2,1)S(1)} %copy-done.3, bf16[512,256]{1,0:T(8,128)(2,1)S(1)} %copy-done.4), kind=kOutput, calls=%fused_computation.30 | convolution fusion | flops 8669626368 | bytes 34148352 | tf_op jit(solution)/shard_map/iq,qxy->ixy/dot_general | solution.py:45
  1106.6 12.2 copy.39
  1118.9 187.9 %all_to_all.34 = bf16[256,16,1024]{2,1,0:T(8,128)(2,1)} all-to-all(bf16[256,16,1024]{2,1,0:T(8,128)(2,1)} %copy.39), channel_id=1, replica_groups=mesh['mesh'=4,'mode'=8] {'mode'}, dimensions={0} | all-to-all | bytes 16777216 | tf_op jit(solution)/shard_map/all_to_all | solution.py:72
  1306.8 8.7 copy.40
  (35 shorter events, 0.1 us)
Async XLA Ops:
  0.0 1023.7 %copy-start = (bf16[3,256,256]{2,1,0:T(8,128)(2,1)S(1)}, bf16[3,256,256]{2,1,0:T(8,128)(2,1)}, u32[]{:S(2)}) copy-start(bf16[3,256,256]{2,1,0:T(8,128)(2,1)} %param.11) | copy-start | bytes 1179652
  0.0 56.6 %slice-start = ((s8[16777216]{0:T(1024)(128)(4,1)}), s8[4194304]{0:T(1024)(128)(4,1)S(1)}, s32[]{:S(2)}) async-start(s8[16777216]{0:T(1024)(128)(4,1)} %bitcast.74), calls=%async_computation.2 | async-start | bytes 8388608
  0.0 56.7 %slice-start.1 = ((s8[16777216]{0:T(1024)(128)(4,1)}), s8[4194304]{0:T(1024)(128)(4,1)S(1)}, s32[]{:S(2)}) async-start(s8[16777216]{0:T(1024)(128)(4,1)} %bitcast.74), calls=%async_computation.3 | async-start | bytes 8388608
  0.0 56.7 %slice-start.2 = ((s8[16777216]{0:T(1024)(128)(4,1)}), s8[4194304]{0:T(1024)(128)(4,1)S(1)}, s32[]{:S(2)}) async-start(s8[16777216]{0:T(1024)(128)(4,1)} %bitcast.74), calls=%async_computation.4 | async-start | bytes 8388608
  0.0 16.6 %copy-start.2 = (bf16[3,16,1024]{2,1,0:T(8,128)(2,1)S(1)}, bf16[3,16,1024]{2,1,0:T(8,128)(2,1)}, u32[]{:S(2)}) copy-start(bf16[3,16,1024]{2,1,0:T(8,128)(2,1)} %param.9) | copy-start | bytes 294916
  16.6 51.5 %copy-start.1 = (bf16[32,128,1024]{2,0,1:T(8,128)(2,1)}, bf16[32,128,1024]{2,0,1:T(8,128)(2,1)S(1)}, u32[]{:S(2)}) copy-start(bf16[32,128,1024]{2,0,1:T(8,128)(2,1)S(1)} %copy.54) | copy-start | bytes 25165828
  45.3 11.4 slice-start.3
  45.4 22.8 %collective-permute-start = (bf16[35,1,1024]{2,0,1:T(8,128)(2,1)S(1)}, bf16[35,1,1024]{2,0,1:T(8,128)(2,1)S(1)}, u32[]{:S(2)}, u32[]{:S(2)}) collective-permute-start(bf16[35,1,1024]{2,0,1:T(8,128)(2,1)S(1)} %get-tuple-element.9), channel_id=1, source_target_pairs={{0,8},{8,16},{16,24},{1,9},{9,17},{17,25},{2,10},{10,18},{18,26},{... | collective-permute-start | bytes 215048 | tf_op jit(solution)/shard_map/ppermute | solution.py:15
  54.5 13.6 %collective-permute-start.1 = (bf16[35,1,1024]{2,0,1:T(8,128)(2,1)S(1)}, bf16[35,1,1024]{2,0,1:T(8,128)(2,1)S(1)}, u32[]{:S(2)}, u32[]{:S(2)}) collective-permute-start(bf16[35,1,1024]{2,0,1:T(8,128)(2,1)S(1)} %get-tuple-element.10), channel_id=1, source_target_pairs={{8,0},{16,8},{24,16},{9,1},{17,9},{25,17},{10,2},{18,10},{26,18},{... | collective-permute-start | bytes 215048 | tf_op jit(solution)/shard_map/ppermute | solution.py:17
  131.2 7.5 slice-start.4
  131.2 7.5 slice-start.5
  134.1 4.6 slice-start.6
  134.1 4.6 slice-start.7
  1023.7 60.0 %copy-start.3 = (bf16[256,512]{1,0:T(8,128)(2,1)S(1)}, bf16[256,512]{1,0:T(8,128)(2,1)}, u32[]{:S(2)}) copy-start(bf16[256,512]{1,0:T(8,128)(2,1)} %param.13) | copy-start | bytes 786436
  1023.7 60.0 %copy-start.4 = (bf16[512,256]{1,0:T(8,128)(2,1)S(1)}, bf16[512,256]{1,0:T(8,128)(2,1)}, u32[]{:S(2)}) copy-start(bf16[512,256]{1,0:T(8,128)(2,1)} %param.12) | copy-start | bytes 786436
  1023.7 60.0 %copy-start.5 = (f32[16,1024]{1,0:T(8,128)S(1)}, f32[16,1024]{1,0:T(8,128)}, u32[]{:S(2)}) copy-start(f32[16,1024]{1,0:T(8,128)} %param.10) | copy-start | bytes 196612
  1023.8 60.0 %copy-start.6 = (f32[512]{0:T(512)S(1)}, f32[512]{0:T(512)}, u32[]{:S(2)}) copy-start(f32[512]{0:T(512)} %param.15) | copy-start | bytes 6148
  1023.8 60.0 %copy-start.7 = (f32[512]{0:T(512)S(1)}, f32[512]{0:T(512)}, u32[]{:S(2)}) copy-start(f32[512]{0:T(512)} %param.14) | copy-start | bytes 6148
where the time goes:
time: 1320 us
  blocking collectives  949 us (72%)
  other arithmetic  140 us (11%)
  local copies, waits for them, and re-layouts  132 us (10%)
  matrix products  82.8 us (6%)
    all_to_all x1, blocking collectives, body(): lax.all_to_all(joined, 'mode', split_axis=1, concat_axis=0, tiled=True)  733 us
    all_to_all x1, blocking collectives, body(): lax.all_to_all(result, 'mode', split_axis=0, concat_axis=1, tiled=True)  188 us
    dot_general x1, matrix products, finish(): jnp.einsum('kij,kjxy->ixy', kl_modes, images, preferred_element_type=jnp....  59.9 us
    mul x2, other arithmetic, conduct(): total = total + 0.5 * (kcentre + kother) * (centre - other)  55.6 us
    convert_element_type x1, other arithmetic, conduct(): return total.astype(jnp.bfloat16)  46.6 us
    slice x2, local copies, waits for them, and re-layouts, body(): node_images = moved[1:]  42.7 us
    all_to_all x1, local copies, waits for them, and re-layouts, body(): lax.all_to_all(joined, 'mode', split_axis=1, concat_axis=0, tiled=True)  30.8 us
    all_gather x1, blocking collectives, body(): kap_rows = lax.all_gather(kappa, 'mode', axis=1, tiled=True)  28.1 us
  transfers between devices with their start and end apart: 2, of which 0 were waited for; matrix products, arithmetic and copies ran while one was open for 1% of the time, Pallas kernels for 0%

commit v1 on v0

--- a/solution.py
+++ b/solution.py
@@ -2,6 +2,29 @@
 import jax.numpy as jnp
 from jax import lax
 from jax.sharding import PartitionSpec as P
+
+
+def cut_along(x, dim, size):
+    shape = x.shape
+    pieces = x.reshape(*shape[:dim], size, shape[dim] // size, *shape[dim + 1 :])
+    return jnp.moveaxis(pieces, dim, 0)
+
+
+def laid_out(blocks, dim):
+    blocks = jnp.moveaxis(blocks, 0, dim)
+    lengths = blocks.shape
+    return blocks.reshape(*lengths[:dim], lengths[dim] * lengths[dim + 1], *lengths[dim + 2 :])
+
+
+def swapped_with_each(x, axis, split_dim, concat_dim):
+    size, here = (lax.axis_size(axis), lax.axis_index(axis))
+    parts = cut_along(x, split_dim, size)
+    done = [parts[here]]
+    for lap in range(1, size):
+        sent = parts[here ^ lap]
+        done.append(lax.ppermute(sent, axis, [(i, i ^ lap) for i in range(size)]))
+    parts = jnp.stack(done)[here ^ jnp.arange(size)]
+    return laid_out(parts, concat_dim)
 
 
 def extended(cells, sides, width):
@@ -58,7 +81,7 @@
     images = conduct(padded[:owned], padded[owned:])
     joined = jnp.concatenate([coarse[None], images], 0)
     joined = joined.reshape((terms + 1) * owned, coarse.shape[1], width)
-    moved = lax.all_to_all(joined, "mode", split_axis=1, concat_axis=0, tiled=True)
+    moved = swapped_with_each(joined, "mode", 1, 0)
     node_rows = moved.shape[1]
     moved = moved.reshape(groups, terms + 1, owned, node_rows, width)
     moved = jnp.transpose(moved, (1, 0, 2, 3, 4)).reshape(

time: 1320 us -> 1470 us (1.11)
  blocking collectives: 949 us -> 385 us
  waiting for transfers between devices: 0.01 us -> 513 us
  local copies, waits for them, and re-layouts: 132 us -> 309 us
    all_to_all x1 -> x0, blocking collectives: 733 us -> none  [body(): lax.all_to_all(joined, 'mode', split_axis=1, concat_axis=0, tiled=True)]
    ppermute x0 -> x7, waiting for transfers between devices: none -> 513 us  [swapped_with_each(): done.append(lax.ppermute(sent, axis, [(i, i ^ lap) for i in range(size)]))]
    all_to_all x1, blocking collectives: 188 us -> 357 us  [body(): lax.all_to_all(result, 'mode', split_axis=0, concat_axis=1, tiled=True)]
    mul x0 -> x8, local copies, waits for them, and re-layouts: none -> 79.2 us  [conduct(): total = total + 0.5 * (kcentre + kother) * (centre - other)]
    gather x0 -> x5, local copies, waits for them, and re-layouts: none -> 56.9 us  [swapped_with_each(): parts = jnp.stack(done)[here ^ jnp.arange(size)]]
    unnamed x34 -> x55, local copies, waits for them, and re-layouts: 28 us -> 63.3 us
    all_to_all x1 -> x0, local copies, waits for them, and re-layouts: 30.8 us -> none  [body(): lax.all_to_all(joined, 'mode', split_axis=1, concat_axis=0, tiled=True)]
    unnamed x2 -> x5, other arithmetic: 0.01 us -> 22.8 us
  transfers between devices with their start and end apart: 2 -> 9, of which waited for: 0 -> 4; matrix products, arithmetic and copies ran while one was open for 1% -> 4% of each run, Pallas kernels for 0% -> 0%
where the time goes in v1:
time: 1470 us; the launch traced here: 1460 us
  waiting for transfers between devices  513 us (35%)
  blocking collectives  385 us (26%)
  local copies, waits for them, and re-layouts  309 us (21%)
  other arithmetic  150 us (10%)
  matrix products  82.7 us (6%)
  starting transfers between devices  19.8 us (1%)
    ppermute x7, waiting for transfers between devices, swapped_with_each(): done.append(lax.ppermute(sent, axis, [(i, i ^ lap) for i in range(size)]))  513 us
    all_to_all x1, blocking collectives, body(): lax.all_to_all(result, 'mode', split_axis=0, concat_axis=1, tiled=True)  357 us
    mul x8, local copies, waits for them, and re-layouts, conduct(): total = total + 0.5 * (kcentre + kother) * (centre - other)  79.2 us
    unnamed x55, local copies, waits for them, and re-layouts  63.3 us
    dot_general x1, matrix products, finish(): jnp.einsum('kij,kjxy->ixy', kl_modes, images, preferred_element_type=jnp....  59.9 us
    gather x5, local copies, waits for them, and re-layouts, swapped_with_each(): parts = jnp.stack(done)[here ^ jnp.arange(size)]  56.9 us
    mul x2, other arithmetic, conduct(): total = total + 0.5 * (kcentre + kother) * (centre - other)  56.5 us
    slice x2, local copies, waits for them, and re-layouts, body(): node_images = moved[1:]  42.7 us
  transfers between devices with their start and end apart: 9, of which 4 were waited for; matrix products, arithmetic and copies ran while one was open for 4% of the time, Pallas kernels for 0%

profile of v1, /device:TPU:1, one launch (start us, length us, event | category | flops | bytes accessed | tf_op | source)
XLA Modules:
  0.0 1460.7 jit_solution(12161880497226152419)
XLA Ops:
  0.0 16.5 %copy.64 = bf16[32,128,1024]{2,0,1:T(8,128)(2,1)S(1)} copy(f32[32,128,1024]{2,1,0:T(8,128)} %param.8) | data formatting | bytes 25165824 | tf_op args[0]
  16.6 28.1 %all_gather.3 = bf16[3,128,1024]{2,1,0:T(8,128)(2,1)S(1)} all-gather(bf16[3,16,1024]{2,1,0:T(8,128)(2,1)S(1)} %copy-done.3), channel_id=1, replica_groups=mesh['mesh'=4,'mode'=8] {'mode'}, dimensions={1}, use_global_device_ids=true | all-gather | bytes 884736 | tf_op jit(solution)/shard_map/all_gather | solution.py:78
  68.1 11.4 copy.46
  79.5 14.2 fusion.11
  93.7 51.8 %fusion.6 = (f32[32,128,1024]{2,0,1:T(8,128)}, f32[32,128,1024]{2,0,1:T(8,128)}, f32[32,128,1024]{2,0,1:T(8,128)}, f32[32,128,1024]{2,0,1:T(8,128)}) fusion(f32[1,32,130,1026]{3,1,2,0:T(8,128)} %fusion.11), kind=kLoop, calls=%fused_computation.19 | loop fusion | flops 16777216 | bytes 150994944 | tf_op jit(solution)/shard_map/mul | solution.py:58
  145.5 19.1 %copy.39 = f32[32,128,1024]{2,1,0:T(8,128)} copy(f32[32,128,1024]{2,0,1:T(8,128)} %get-tuple-element.14) | data formatting | bytes 33554432 | tf_op jit(solution)/shard_map/mul | solution.py:58
  164.7 19.0 %copy.41 = f32[32,128,1024]{2,1,0:T(8,128)} copy(f32[32,128,1024]{2,0,1:T(8,128)S(1)} %copy-done.2) | data formatting | bytes 33554432 | tf_op jit(solution)/shard_map/mul | solution.py:58
  183.7 18.3 %copy.43 = f32[32,128,1024]{2,1,0:T(8,128)} copy(f32[32,128,1024]{2,0,1:T(8,128)} %get-tuple-element.15) | data formatting | bytes 33554432 | tf_op jit(solution)/shard_map/mul | solution.py:58
  202.0 19.1 %copy.45 = f32[32,128,1024]{2,1,0:T(8,128)} copy(f32[32,128,1024]{2,0,1:T(8,128)S(1)} %bitcast.104) | data formatting | bytes 33554432 | tf_op jit(solution)/shard_map/mul | solution.py:58
  232.5 30.4 %add_convert_fusion = bf16[3,32,128,1024]{3,2,1,0:T(8,128)(2,1)} fusion(f32[32,128,1024]{2,1,0:T(8,128)} %copy.45, f32[3,128,1024]{2,1,0:T(8,128)S(1)} %copy.44, f32[32,128,1024]{2,1,0:T(8,128)} %copy.43, f32[3,128,1024]{2,1,0:T(8,128)S(1)} %copy.42, f32[32,128,1024]{2,1,0:T(8,128)} %copy.41, f32[3,128,1024]{2,1,0:T(8,128)S(1)} %copy.40, ...), kind=kLoop, calls=%fused_computation.3 | loop fusion | flops 100663296 | bytes 98566144 | tf_op jit(solution)/shard_map/convert_element_type | solution.py:59
  262.9 23.1 %pad_maximum_fusion = bf16[4,32,128,1024]{3,2,1,0:T(8,128)(2,1)} fusion(bf16[3,32,128,1024]{3,2,1,0:T(8,128)(2,1)} %add_convert_fusion, bf16[1,32,128,1024]{3,2,1,0:T(8,128)(2,1)} %copy.46), kind=kLoop, calls=%fused_computation.4 | loop fusion | flops 16777216 | bytes 67108864 | tf_op jit(solution)/shard_map/concatenate | solution.py:82
  286.0 20.6 %dynamic-slice_bitcast_fusion = (bf16[128,16,1024]{2,1,0:T(8,128)(2,1)}, bf16[128,16,1024]{2,1,0:T(8,128)(2,1)}, bf16[128,16,1024]{2,1,0:T(8,128)(2,1)}, bf16[12...) fusion(bf16[128,8,16,1024]{3,2,1,0:T(8,128)(2,1)} %bitcast.101,, ...), kind=kLoop, calls=%fused_computation.43 | loop fusion | bytes 58720284 | tf_op jit(solution)/shard_map/squeeze | solution.py:24
  312.7 85.0 %collective-permute-done.2 = bf16[128,16,1024]{2,1,0:T(8,128)(2,1)} collective-permute-done((bf16[128,16,1024]{2,1,0:T(8,128)(2,1)}, bf16[128,16,1024]{2,1,0:T(8,128)(2,1)}, u32[]{:S(2)}, u32[]{:S(2)}) %collective-permute-start.2) | collective-permute-done | bytes 4194336 | tf_op jit(solution)/shard_map/ppermute | solution.py:25
  400.2 178.9 %collective-permute-done.3 = bf16[128,16,1024]{2,1,0:T(8,128)(2,1)} collective-permute-done((bf16[128,16,1024]{2,1,0:T(8,128)(2,1)}, bf16[128,16,1024]{2,1,0:T(8,128)(2,1)}, u32[]{:S(2)}, u32[]{:S(2)}) %collective-permute-start.3) | collective-permute-done | bytes 4194336 | tf_op jit(solution)/shard_map/ppermute | solution.py:25
  594.3 71.5 %collective-permute-done.4 = bf16[128,16,1024]{2,1,0:T(8,128)(2,1)} collective-permute-done((bf16[128,16,1024]{2,1,0:T(8,128)(2,1)}, bf16[128,16,1024]{2,1,0:T(8,128)(2,1)}, u32[]{:S(2)}, u32[]{:S(2)}) %collective-permute-start.4) | collective-permute-done | bytes 4194336 | tf_op jit(solution)/shard_map/ppermute | solution.py:25
  675.9 177.4 %collective-permute-done.6 = bf16[128,16,1024]{2,1,0:T(8,128)(2,1)} collective-permute-done((bf16[128,16,1024]{2,1,0:T(8,128)(2,1)}, bf16[128,16,1024]{2,1,0:T(8,128)(2,1)}, u32[]{:S(2)}, u32[]{:S(2)}) %collective-permute-start.6) | collective-permute-done | bytes 4194336 | tf_op jit(solution)/shard_map/ppermute | solution.py:25
  868.3 18.8 %fusion.49 = (bf16[8,128,16,384]{3,2,1,0:T(8,128)(2,1)}, bf16[8,128,16,384]{3,2,1,0:T(8,128)(2,1)}) fusion(bf16[8,128,16,1024]{3,2,1,0:T(8,128)(2,1)} %bitcast_dynamic-update-slice_fusion), kind=kLoop, calls=%fused_computation.82 | loop fusion | bytes 50331648 | tf_op jit(solution)/shard_map/gather | solution.py:26
  925.2 22.8 %pad_maximum_fusion.1 = bf16[8,128,16,1024]{3,2,1,0:T(8,128)(2,1)} fusion(bf16[8,128,16,256]{3,2,1,0:T(8,128)(2,1)} %gather_fusion.2, bf16[8,128,16,384]{3,2,1,0:T(8,128)(2,1)} %gather_fusion.1, bf16[8,128,16,384]{3,2,1,0:T(8,128)(2,1)} %gather_fusion), kind=kLoop, calls=%fused_computation.5 | loop fusion | flops 100663296 | bytes 67108864
  948.0 21.3 %slice.86 = bf16[3,8,32,16,1024]{4,3,2,0,1:T(8,128)(2,1)} slice(bf16[4,8,32,16,1024]{4,3,2,0,1:T(8,128)(2,1)} %bitcast.99), slice={[1:4], [0:8], [0:32], [0:16], [0:1024]} | slice | bytes 50331648 | tf_op jit(solution)/shard_map/slice | solution.py:91
  978.0 21.4 %copy.48 = bf16[3,8,32,16,1024]{4,3,2,1,0:T(8,128)(2,1)} copy(bf16[3,8,32,16,1024]{4,3,2,0,1:T(8,128)(2,1)} %slice.86) | data formatting | bytes 50331648 | tf_op jit(solution)/shard_map/slice | solution.py:91
  999.4 59.9 %fusion = f32[16,1024,256,1]{2,1,3,0:T(8,128)} fusion(bf16[3,256,16,1024]{3,2,1,0:T(8,128)(2,1)} %bitcast.111, bf16[3,256,256]{2,1,0:T(8,128)(2,1)S(1)} %copy-done), kind=kOutput, calls=%fused_computation.9 | convolution fusion | flops 6442450944 | bytes 42336256 | tf_op jit(solution)/shard_map/kij,kjxy->ixy/dot_general | solution.py:63
  1059.4 22.9 %fusion.23 = bf16[256,16,1024]{0,2,1:T(8,128)(2,1)} fusion(f32[16,1024,256,1]{2,1,3,0:T(8,128)} %fusion, f32[512]{0:T(512)S(1)} %copy-done.7, f32[512]{0:T(512)S(1)} %copy-done.8, bf16[256,16,1024]{2,1,0:T(8,128)(2,1)} %bitcast.112, f32[16,1024]{1,0:T(8,128)S(1)} %copy-done.6, bf16[256,512]{1,0:T(8,128)(2,1)S(1)} %copy-done.4, ...), kind=kOutput, calls=%fused_computation.34 | convolution fusion | flops 8669626368 | bytes 34148352 | tf_op jit(solution)/shard_map/iq,qxy->ixy/dot_general | solution.py:68
  1082.2 12.2 copy.50
  1094.5 357.2 %all_to_all.18 = bf16[256,16,1024]{2,1,0:T(8,128)(2,1)} all-to-all(bf16[256,16,1024]{2,1,0:T(8,128)(2,1)} %copy.50), channel_id=1, replica_groups=mesh['mesh'=4,'mode'=8] {'mode'}, dimensions={0} | all-to-all | bytes 16777216 | tf_op jit(solution)/shard_map/all_to_all | solution.py:95
  (89 shorter events, 139.1 us)
Async XLA Ops:
  0.0 999.4 %copy-start = (bf16[3,256,256]{2,1,0:T(8,128)(2,1)S(1)}, bf16[3,256,256]{2,1,0:T(8,128)(2,1)}, u32[]{:S(2)}) copy-start(bf16[3,256,256]{2,1,0:T(8,128)(2,1)} %param.11) | copy-start | bytes 1179652
  0.0 56.6 %slice-start.6 = ((s8[16777216]{0:T(1024)(128)(4,1)}), s8[4194304]{0:T(1024)(128)(4,1)S(1)}, s32[]{:S(2)}) async-start(s8[16777216]{0:T(1024)(128)(4,1)} %bitcast.105), calls=%async_computation.7 | async-start | bytes 8388608
  0.0 56.7 %slice-start.7 = ((s8[16777216]{0:T(1024)(128)(4,1)}), s8[4194304]{0:T(1024)(128)(4,1)S(1)}, s32[]{:S(2)}) async-start(s8[16777216]{0:T(1024)(128)(4,1)} %bitcast.105), calls=%async_computation.8 | async-start | bytes 8388608
  0.0 56.7 %slice-start.8 = ((s8[16777216]{0:T(1024)(128)(4,1)}), s8[4194304]{0:T(1024)(128)(4,1)S(1)}, s32[]{:S(2)}) async-start(s8[16777216]{0:T(1024)(128)(4,1)} %bitcast.105), calls=%async_computation.9 | async-start | bytes 8388608
  16.6 51.5 %copy-start.1 = (bf16[32,128,1024]{2,0,1:T(8,128)(2,1)}, bf16[32,128,1024]{2,0,1:T(8,128)(2,1)S(1)}, u32[]{:S(2)}) copy-start(bf16[32,128,1024]{2,0,1:T(8,128)(2,1)S(1)} %copy.64) | copy-start | bytes 25165828
  45.4 34.2 %collective-permute-start = (bf16[35,1,1024]{2,0,1:T(8,128)(2,1)S(1)}, bf16[35,1,1024]{2,0,1:T(8,128)(2,1)S(1)}, u32[]{:S(2)}, u32[]{:S(2)}) collective-permute-start(bf16[35,1,1024]{2,0,1:T(8,128)(2,1)S(1)} %get-tuple-element.18), channel_id=1, source_target_pairs={{0,8},{8,16},{16,24},{1,9},{9,17},{17,25},{2,10},{10,18},{18,26},{... | collective-permute-start | bytes 215048 | tf_op jit(solution)/shard_map/ppermute | solution.py:38
  54.5 25.0 %collective-permute-start.1 = (bf16[35,1,1024]{2,0,1:T(8,128)(2,1)S(1)}, bf16[35,1,1024]{2,0,1:T(8,128)(2,1)S(1)}, u32[]{:S(2)}, u32[]{:S(2)}) collective-permute-start(bf16[35,1,1024]{2,0,1:T(8,128)(2,1)S(1)} %get-tuple-element.19), channel_id=1, source_target_pairs={{8,0},{16,8},{24,16},{9,1},{17,9},{25,17},{10,2},{18,10},{26,18},{... | collective-permute-start | bytes 215048 | tf_op jit(solution)/shard_map/ppermute | solution.py:40
  145.5 19.1 %copy-start.2 = (f32[32,128,1024]{2,0,1:T(8,128)S(1)}, f32[32,128,1024]{2,0,1:T(8,128)}, u32[]{:S(2)}) copy-start(f32[32,128,1024]{2,0,1:T(8,128)} %get-tuple-element.16) | copy-start | bytes 50331652
  164.7 37.3 %slice-start.2 = ((s8[16777216]{0:T(1024)(128)(4,1)}), s8[4194304]{0:T(1024)(128)(4,1)S(1)}, s32[]{:S(2)}) async-start(s8[16777216]{0:T(1024)(128)(4,1)} %bitcast.103), calls=%async_computation.3 | async-start | bytes 8388608
  164.7 37.3 %slice-start.3 = ((s8[16777216]{0:T(1024)(128)(4,1)}), s8[4194304]{0:T(1024)(128)(4,1)S(1)}, s32[]{:S(2)}) async-start(s8[16777216]{0:T(1024)(128)(4,1)} %bitcast.103), calls=%async_computation.4 | async-start | bytes 8388608
  183.7 37.4 %slice-start = ((s8[8388608]{0:T(1024)(128)(4,1)}), s8[4194304]{0:T(1024)(128)(4,1)S(1)}, s32[]{:S(2)}) async-start(s8[8388608]{0:T(1024)(128)(4,1)} %bitcast.97), calls=%async_computation.1 | async-start | bytes 8388608
  202.0 19.1 %slice-start.1 = ((s8[8388608]{0:T(1024)(128)(4,1)}), s8[4194304]{0:T(1024)(128)(4,1)S(1)}, s32[]{:S(2)}) async-start(s8[8388608]{0:T(1024)(128)(4,1)} %bitcast.97), calls=%async_computation.2 | async-start | bytes 8388608
  306.6 91.1 %collective-permute-start.2 = (bf16[128,16,1024]{2,1,0:T(8,128)(2,1)}, bf16[128,16,1024]{2,1,0:T(8,128)(2,1)}, u32[]{:S(2)}, u32[]{:S(2)}) collective-permute-start(bf16[128,16,1024]{2,1,0:T(8,128)(2,1)} %get-tuple-element.13), channel_id=1, source_target_pairs={{0,1},{1,0},{2,3},{3,2},{4,5},{5,4},{6,7},{7,6},{8,9},{9,8},{10,11... | collective-permute-start | bytes 12582920 | tf_op jit(solution)/shard_map/ppermute | solution.py:25
  307.9 271.2 %collective-permute-start.3 = (bf16[128,16,1024]{2,1,0:T(8,128)(2,1)}, bf16[128,16,1024]{2,1,0:T(8,128)(2,1)}, u32[]{:S(2)}, u32[]{:S(2)}) collective-permute-start(bf16[128,16,1024]{2,1,0:T(8,128)(2,1)} %get-tuple-element.12), channel_id=1, source_target_pairs={{0,2},{1,3},{2,0},{3,1},{4,6},{5,7},{6,4},{7,5},{8,10},{9,11},{10,... | collective-permute-start | bytes 12582920 | tf_op jit(solution)/shard_map/ppermute | solution.py:25
  307.9 357.8 %collective-permute-start.4 = (bf16[128,16,1024]{2,1,0:T(8,128)(2,1)}, bf16[128,16,1024]{2,1,0:T(8,128)(2,1)}, u32[]{:S(2)}, u32[]{:S(2)}) collective-permute-start(bf16[128,16,1024]{2,1,0:T(8,128)(2,1)} %get-tuple-element.11), channel_id=1, source_target_pairs={{0,3},{1,2},{2,1},{3,0},{4,7},{5,6},{6,5},{7,4},{8,11},{9,10},{10,... | collective-permute-start | bytes 12582920 | tf_op jit(solution)/shard_map/ppermute | solution.py:25
  309.3 361.5 %collective-permute-start.5 = (bf16[128,16,1024]{2,1,0:T(8,128)(2,1)}, bf16[128,16,1024]{2,1,0:T(8,128)(2,1)}, u32[]{:S(2)}, u32[]{:S(2)}) collective-permute-start(bf16[128,16,1024]{2,1,0:T(8,128)(2,1)} %get-tuple-element.10), channel_id=1, source_target_pairs={{0,4},{1,5},{2,6},{3,7},{4,0},{5,1},{6,2},{7,3},{8,12},{9,13},{10,... | collective-permute-start | bytes 12582920 | tf_op jit(solution)/shard_map/ppermute | solution.py:25
  311.2 542.0 %collective-permute-start.6 = (bf16[128,16,1024]{2,1,0:T(8,128)(2,1)}, bf16[128,16,1024]{2,1,0:T(8,128)(2,1)}, u32[]{:S(2)}, u32[]{:S(2)}) collective-permute-start(bf16[128,16,1024]{2,1,0:T(8,128)(2,1)} %get-tuple-element.9), channel_id=1, source_target_pairs={{0,5},{1,4},{2,7},{3,6},{4,1},{5,0},{6,3},{7,2},{8,13},{9,12},{10,... | collective-permute-start | bytes 12582920 | tf_op jit(solution)/shard_map/ppermute | solution.py:25
  397.7 460.6 %collective-permute-start.7 = (bf16[128,16,1024]{2,1,0:T(8,128)(2,1)}, bf16[128,16,1024]{2,1,0:T(8,128)(2,1)}, u32[]{:S(2)}, u32[]{:S(2)}) collective-permute-start(bf16[128,16,1024]{2,1,0:T(8,128)(2,1)} %get-tuple-element.8), channel_id=1, source_target_pairs={{0,6},{1,7},{2,4},{3,5},{4,2},{5,3},{6,0},{7,1},{8,14},{9,15},{10,... | collective-permute-start | bytes 12582920 | tf_op jit(solution)/shard_map/ppermute | solution.py:25
  579.1 284.2 %collective-permute-start.8 = (bf16[128,16,1024]{2,1,0:T(8,128)(2,1)}, bf16[128,16,1024]{2,1,0:T(8,128)(2,1)}, u32[]{:S(2)}, u32[]{:S(2)}) collective-permute-start(bf16[128,16,1024]{2,1,0:T(8,128)(2,1)} %get-tuple-element.7), channel_id=1, source_target_pairs={{0,7},{1,6},{2,5},{3,4},{4,3},{5,2},{6,1},{7,0},{8,15},{9,14},{10,... | collective-permute-start | bytes 12582920 | tf_op jit(solution)/shard_map/ppermute | solution.py:25
  999.4 59.9 %copy-start.4 = (bf16[256,512]{1,0:T(8,128)(2,1)S(1)}, bf16[256,512]{1,0:T(8,128)(2,1)}, u32[]{:S(2)}) copy-start(bf16[256,512]{1,0:T(8,128)(2,1)} %param.13) | copy-start | bytes 786436
  999.4 59.9 %copy-start.5 = (bf16[512,256]{1,0:T(8,128)(2,1)S(1)}, bf16[512,256]{1,0:T(8,128)(2,1)}, u32[]{:S(2)}) copy-start(bf16[512,256]{1,0:T(8,128)(2,1)} %param.12) | copy-start | bytes 786436
  999.4 59.9 %copy-start.6 = (f32[16,1024]{1,0:T(8,128)S(1)}, f32[16,1024]{1,0:T(8,128)}, u32[]{:S(2)}) copy-start(f32[16,1024]{1,0:T(8,128)} %param.10) | copy-start | bytes 196612
  999.4 59.9 %copy-start.7 = (f32[512]{0:T(512)S(1)}, f32[512]{0:T(512)}, u32[]{:S(2)}) copy-start(f32[512]{0:T(512)} %param.15) | copy-start | bytes 6148
  999.4 59.9 %copy-start.8 = (f32[512]{0:T(512)S(1)}, f32[512]{0:T(512)}, u32[]{:S(2)}) copy-start(f32[512]{0:T(512)} %param.14) | copy-start | bytes 6148
  (8 other events, 92.7 us)
